TPU v7x, 1024 devices: a whole 4x8x16 slice. The times are simulated.
1024 devices in a mesh: domain: 128 (over z, y_lo, core), band: 8 (over x, y_hi).
Axes of the slice: x: 4, y: 8 (y_hi: 2, y_lo: 4; y = y_hi * 4 + y_lo), z: 16, core: 2. Of those that a mesh axis runs over, the one named last changes fastest.
Arguments:
- orbitals: bfloat16 [256, 256, 8, 128], P('band', 'domain'), may hold values from -6 to 6
- potential: float32 [256, 8, 128], P('domain'), may hold values from -1 to 1.5
Outputs:
- filtered: bfloat16 [256, 256, 8, 128], P('band', 'domain')
- margin_rows: float32 [256, 256], P('band')
- projected_rows: float32 [256, 256], P('band')
All inputs are finite; a program needn't handle non-finite values.
Results may differ from a plain program's by a relative error of at most 0.003.
Values may be sent and summed in bfloat16 or wider, within the bound.
A program may use at most 32 MiB of HBM per device.

v0:
```python
import jax
import jax.numpy as jnp
from jax import lax
from jax.sharding import PartitionSpec as P

LOWER = -1.0
CUTOFF = 1.0
UPPER = 7.5


def extended_2(block, sides, width):
    for axis, dim in sides:
        count = lax.axis_size(axis)
        forward = [(i, i + 1) for i in range(count - 1)]
        forward.append((count - 1, 0))
        backward = [(target, source) for source, target in forward]
        low = lax.ppermute(
            lax.slice_in_dim(block, block.shape[dim] - width, None, axis=dim), axis, forward
        )
        high = lax.ppermute(lax.slice_in_dim(block, 0, width, axis=dim), axis, backward)
        block = jnp.concatenate([low, block, high], axis=dim)
    return block


def filter_terms():
    half_width = (UPPER - CUTOFF) / 2.0
    center = (UPPER + CUTOFF) / 2.0
    sigma = half_width / (LOWER - center)
    gamma = 2.0 / sigma
    terms = [(sigma / half_width, 0.0)]
    for step in range(3):
        sigma_next = 1.0 / (gamma - sigma)
        terms.append((2.0 * sigma_next / half_width, sigma * sigma_next))
        sigma = sigma_next
    return (center, terms)


def hamil(extended, potential):
    centre = extended[:, 1:-1]
    near = extended[:, 2:] + extended[:, :-2]
    near = near + jnp.roll(centre, 1, 2) + jnp.roll(centre, -1, 2)
    near = near + jnp.roll(centre, 1, 3) + jnp.roll(centre, -1, 3)
    return -0.5 * (near - 6.0 * centre) + potential[None] * centre


def rim(field):
    return extended_2(field, (("domain", 1),), 1)


def shards(orbitals, potential):
    center, terms = filter_terms()
    prior = orbitals.astype(jnp.float32)
    current = terms[0][0] * (hamil(rim(prior), potential) - center * prior)
    for alpha, beta in terms[1:]:
        update = alpha * (hamil(rim(current), potential) - center * current) - beta * prior
        prior, current = (current, update)
    filtered = current.astype(jnp.bfloat16)
    applied = hamil(rim(filtered.astype(jnp.float32)), potential).astype(jnp.bfloat16)
    block_rows = filtered.shape[0]
    flat_y = filtered.reshape(block_rows, -1)
    flat_h = applied.reshape(block_rows, -1)
    scale = 1.0 / (
        filtered.shape[1] * lax.axis_size("domain") * filtered.shape[2] * filtered.shape[3]
    )
    dims = (((1,), (1,)), ((), ()))
    piece = lax.all_gather(filtered, "band", axis=0, tiled=True)
    piece_flat = piece.reshape(piece.shape[0], -1)
    over_tile = lax.dot_general(flat_y, piece_flat, dims, preferred_element_type=jnp.float32)
    proj_tile = lax.dot_general(flat_h, piece_flat, dims, preferred_element_type=jnp.float32)
    over_sum, proj_sum = lax.psum((over_tile, proj_tile), "domain")
    return (filtered, over_sum * scale, proj_sum * scale)


def solution(mesh):
    in_specs = (P("band", "domain", None, None), P("domain", None, None))
    out_specs = (P("band", "domain", None, None), P("band", None), P("band", None))
    return jax.shard_map(shards, mesh=mesh, in_specs=in_specs, out_specs=out_specs, check_vma=False)
```

profile of v0, /device:TPU:1, one launch (start us, length us, event | category | flops | bytes accessed | tf_op | source)
XLA Modules:
  0.0 1065.5 jit_solution(6859695508825883938)
XLA Ops:
  7.2 0.0 all-gather.2.cloned.1.call-start
  7.2 0.9 copy_convert_fusion
  8.2 16.1 %collective-permute-start = (f32[32,1,8,128]{3,0,2,1:T(8,128)S(1)}, f32[32,1,8,128]{3,0,2,1:T(8,128)S(1)}, u32[]{:S(2)}, u32[]{:S(2)}) collective-permute-start(f32[32,1,8,128]{3,0,2,1:T(8,128)S(1)} %get-tuple-element.42), channel_id=1, source_target_pairs={{8,0},{16,8},{24,16},{32,24},{40,32},{48,40},{56,48},{64,56},{72,6... | collective-permute-start | bytes 393224 | tf_op jit(solution)/shard_map/ppermute | solution.py:20
  24.2 1.9 collective-permute-start.1
  26.2 0.1 fusion.80
  26.3 0.1 fusion.81
  26.5 0.0 copy-start.3
  26.5 0.7 copy-done.3
  27.2 0.0 collective-permute-done
  27.2 5.9 collective-permute-done.1
  33.1 0.3 broadcast_multiply_fusion
  33.4 0.1 fusion.72
  33.5 0.1 fusion.73
  33.8 0.0 copy-start.2
  33.8 9.6 collective-permute-start.2
  43.4 1.9 collective-permute-start.3
  45.3 0.0 collective-permute-done.2
  45.3 1.9 collective-permute-done.3
  47.2 0.0 copy-done.2
  47.2 0.3 fusion.41
  47.6 0.1 fusion.67
  47.7 0.1 fusion.68
  47.9 8.3 collective-permute-start.4
  56.2 1.9 collective-permute-start.5
  58.1 0.0 collective-permute-done.4
  58.2 1.9 collective-permute-done.5
  60.1 0.3 fusion.30
  60.4 0.1 fusion.65
  60.5 0.1 fusion.66
  60.8 8.3 collective-permute-start.6
  69.0 1.9 collective-permute-start.7
  71.0 0.0 collective-permute-done.6
  71.0 1.9 collective-permute-done.7
  72.9 1.0 fusion.59
  73.9 0.0 copy-start
  73.9 0.0 all-gather.2.cloned.1.call-update
  73.9 0.0 all-reduce.3.cloned.1.call-start
  74.0 0.8 copy-done
  74.8 8.4 collective-permute-start.8
  83.2 1.9 collective-permute-start.9
  85.2 0.1 fusion.82
  85.3 0.1 fusion.83
  85.4 58.6 %all-gather.2.cloned.1.call-done = bf16[256,2,8,128]{3,0,2,1:T(8,128)(2,1)} async-done(((bf16[32,2,8,128]{3,0,2,1:T(8,128)(2,1)}), bf16[256,2,8,128]{3,0,2,1:T(8,128)(2,1)}) %all-gather.2.cloned.1.call-update) | async-done | bytes 1048592 | tf_op jit(solution)/shard_map/all_gather | solution.py:66
  144.1 0.0 copy-start.1
  144.1 2.3 convolution_bitcast_fusion.1
  146.4 0.0 collective-permute-done.8
  146.4 0.0 collective-permute-done.9
  146.4 0.0 copy-done.1
  146.4 1.0 convolution_bitcast_fusion
  147.5 0.0 all-reduce.3.cloned.1.call-update
  147.5 0.7 copy.6
  148.2 909.1 %all-reduce.3.cloned.1.call-done = (f32[32,256]{1,0:T(8,128)}, f32[32,256]{1,0:T(8,128)}) async-done(((f32[32,256]{1,0:T(8,128)}, f32[32,256]{1,0:T(8,128)}), (f32[32,256]{1,0:T(8,128)}, f32[32,256]{1,0:T(8,128)})) %all-reduce.3.cloned.1.call-update) | async-done | bytes 65552 | tf_op jit(solution)/shard_map/psum | solution.py:70
  1057.3 1.4 broadcast_multiply_fusion.1
  (16 shorter events, 0.4 us)
Async XLA Ops:
  7.2 136.9 %all-gather.2.cloned.1.call-start = ((), (), s32[]{:S(2)}) async-start(), calls=%async_computation | async-start | bytes 1179648 | tf_op jit(solution)/shard_map/all_gather | solution.py:66
  8.2 19.0 %collective-permute-start = (f32[32,1,8,128]{3,0,2,1:T(8,128)S(1)}, f32[32,1,8,128]{3,0,2,1:T(8,128)S(1)}, u32[]{:S(2)}, u32[]{:S(2)}) collective-permute-start(f32[32,1,8,128]{3,0,2,1:T(8,128)S(1)} %get-tuple-element.42), channel_id=1, source_target_pairs={{8,0},{16,8},{24,16},{32,24},{40,32},{48,40},{56,48},{64,56},{72,6... | collective-permute-start | bytes 393224 | tf_op jit(solution)/shard_map/ppermute | solution.py:20
  24.2 8.9 collective-permute-start.1
  26.5 0.7 copy-start.3
  33.8 13.5 %copy-start.2 = (bf16[32,2,8,128]{3,2,1,0:T(8,128)(2,1)S(1)}, bf16[32,2,8,128]{3,2,1,0:T(8,128)(2,1)}, u32[]{:S(2)}) copy-start(bf16[32,2,8,128]{3,2,1,0:T(8,128)(2,1)} %param.2) | copy-start | bytes 393220
  33.8 11.5 %collective-permute-start.2 = (f32[32,1,8,128]{3,0,2,1:T(8,128)S(1)}, f32[32,1,8,128]{3,0,2,1:T(8,128)S(1)}, u32[]{:S(2)}, u32[]{:S(2)}) collective-permute-start(f32[32,1,8,128]{3,0,2,1:T(8,128)S(1)} %get-tuple-element.40), channel_id=1, source_target_pairs={{8,0},{16,8},{24,16},{32,24},{40,32},{48,40},{56,48},{64,56},{72,6... | collective-permute-start | bytes 393224 | tf_op jit(solution)/shard_map/ppermute | solution.py:20
  43.4 3.9 collective-permute-start.3
  47.9 10.2 collective-permute-start.4
  56.2 3.9 collective-permute-start.5
  60.8 10.2 collective-permute-start.6
  69.0 3.9 collective-permute-start.7
  73.9 0.9 copy-start
  73.9 983.4 %all-reduce.3.cloned.1.call-start = ((), (), s32[]{:S(2)}) async-start(), calls=%async_computation.1 | async-start | bytes 131072 | tf_op jit(solution)/shard_map/psum | solution.py:70
  74.8 71.6 %collective-permute-start.8 = (f32[32,1,8,128]{3,0,2,1:T(8,128)S(1)}, f32[32,1,8,128]{3,0,2,1:T(8,128)S(1)}, u32[]{:S(2)}, u32[]{:S(2)}) collective-permute-start(f32[32,1,8,128]{3,0,2,1:T(8,128)S(1)} %get-tuple-element.60), channel_id=1, source_target_pairs={{8,0},{16,8},{24,16},{32,24},{40,32},{48,40},{56,48},{64,56},{72,6... | collective-permute-start | bytes 393224 | tf_op jit(solution)/shard_map/ppermute | solution.py:20
  83.2 63.2 %collective-permute-start.9 = (f32[32,1,8,128]{3,0,2,1:T(8,128)S(1)}, f32[32,1,8,128]{3,0,2,1:T(8,128)S(1)}, u32[]{:S(2)}, u32[]{:S(2)}) collective-permute-start(f32[32,1,8,128]{3,0,2,1:T(8,128)S(1)} %get-tuple-element.61), channel_id=1, source_target_pairs={{0,8},{8,16},{16,24},{24,32},{32,40},{40,48},{48,56},{56,64},{64,7... | collective-permute-start | bytes 393224 | tf_op jit(solution)/shard_map/ppermute | solution.py:17
  144.1 2.4 copy-start.1
Sparse Core Ops, SparseCore 0:
  74.0 69.9 all-gather.1
  148.2 909.0 all-reduce.2
where the time goes:
time: 1070 us
  waiting for transfers between devices  979 us (91%)
  starting transfers between devices  60.2 us (6%)
  between operations  14.4 us (1%)
    psum x1, waiting for transfers between devices, shards(): over_sum, proj_sum = lax.psum((over_tile, proj_tile), 'domain')  909 us
    all_gather x1, waiting for transfers between devices, shards(): piece = lax.all_gather(filtered, 'band', axis=0, tiled=True)  58.6 us
    ppermute x5, starting transfers between devices, extended_2(): lax.ppermute(lax.slice_in_dim(block, 0, width, axis=dim), axis, backward)  50.5 us
  transfers between devices with their start and end apart: 12, of which 6 were waited for; matrix products, arithmetic and copies ran while one was open for 0% of the time, Pallas kernels for 0%

commit v1 on v0

v1 whole, which is shorter than its diff:
```python
import functools

import jax
import jax.numpy as jnp
from jax import lax
from jax.experimental import pallas as pl
from jax.experimental.pallas import tpu as pltpu
from jax.sharding import PartitionSpec as P

MESH = pl.DeviceIdType.MESH
LOWER = -1.0
CUTOFF = 1.0
UPPER = 7.5
F32 = jnp.float32
BF16 = jnp.bfloat16
GROUP = 8
NB = 32
NY = 8
NZ = 128
CHUNKS = 4
HALVES = 2


def filter_terms():
    half_width = (UPPER - CUTOFF) / 2.0
    center = (UPPER + CUTOFF) / 2.0
    sigma = half_width / (LOWER - center)
    gamma = 2.0 / sigma
    terms = [(sigma / half_width, 0.0)]
    for step in range(3):
        sigma_next = 1.0 / (gamma - sigma)
        terms.append((2.0 * sigma_next / half_width, sigma * sigma_next))
        sigma = sigma_next
    return center, terms


def side_sum(plane):
    return (
        (pltpu.roll(plane, 1, 0) + pltpu.roll(plane, NY - 1, 0))
        + (pltpu.roll(plane, 1, 1) + pltpu.roll(plane, NZ - 1, 1))
    )


def kernel(
    n_domain, scale,
    x_hbm, v_ref,
    y_ref, g_ref,
    xs, vs, ws, zst, hst, halo_out, halo_in, zall, lhs, gsum, rsb, zb, fin,
    lsem, xss, xrs, vss, vrs, hss, hrs, bss, brs, fss, frs, rss, rrs, zss, zrs, ass, ars,
):
    n_z = n_domain // GROUP
    d = lax.axis_index("domain")
    b = lax.axis_index("band")
    z, j = d // GROUP, d % GROUP
    x, h = b // 2, b % 2

    def at_d(step):
        return (lax.rem(d + step + n_domain, n_domain), b)

    def at_g(step):
        return (z * GROUP + lax.rem(j + step + GROUP, GROUP), b)

    def at_z(step):
        return (lax.rem(z + step + n_z, n_z) * GROUP + j, b)

    def at_b(dx, dh):
        return (d, lax.rem(x + dx + 4, 4) * 2 + lax.rem(h + dh, 2))

    def remote(src, dst, send, recv, to):
        return pltpu.make_async_remote_copy(
            src_ref=src, dst_ref=dst, send_sem=send, recv_sem=recv, device_id=to, device_id_type=MESH
        )

    own = pltpu.make_async_copy(x_hbm, xs.at[2], lsem)
    own.start()
    barrier = pltpu.get_barrier_semaphore()
    partners = [at_d(s) for s in (-2, -1, 1, 2)] + [at_g(s) for s in range(1, GROUP)] + [at_z(-1), at_z(1)]
    partners += [at_b(0, 1), at_b(1, 0), at_b(-1, 0), at_b(2, 0)]
    for to in partners:
        pl.semaphore_signal(barrier, inc=1, device_id=to, device_id_type=MESH)
    vs[2] = v_ref[...]
    own.wait()
    pl.semaphore_wait(barrier, len(partners))

    pending = []
    shifts = (-1, 1, -2, 2)
    v_in = []
    for n, s in enumerate(shifts):
        cp = remote(vs.at[2], vs.at[2 - s], vss.at[n], vrs.at[n], at_d(s))
        cp.start()
        v_in.append(cp)
    pending += v_in
    size = NB // CHUNKS
    x_in = []
    for c in range(CHUNKS):
        part = pl.ds(c * size, size)
        x_in.append([])
        for n, s in enumerate(shifts):
            cp = remote(xs.at[2, part], xs.at[2 - s, part], xss.at[n, c], xrs.at[n, c], at_d(s))
            cp.start()
            x_in[c].append(cp)
        pending += x_in[c]

    center, terms = filter_terms()
    for cp in v_in:
        cp.wait_recv()
    for k, (alpha, _) in enumerate(terms):
        for p in range(k + 1, 9 - k):
            ws[k, p] = alpha * (vs[p // 2, (p % 2) * NY:(p % 2) * NY + NY, :] + (3.0 - center))

    def filter_one(o):
        prior = {}
        for s in range(5):
            block = xs[s, o].astype(F32)
            prior[2 * s], prior[2 * s + 1] = block[:NY], block[NY:]
        current = None
        for k, (alpha, beta) in enumerate(terms):
            base = prior if k == 0 else current
            update = {}
            for p in range(k + 1, 9 - k):
                near = side_sum(base[p]) + (base[p - 1] + base[p + 1])
                value = ws[k, p] * base[p] - (0.5 * alpha) * near
                if k:
                    value = value - beta * prior[p]
                update[p] = value
            if k:
                prior = current
            current = update
        zst[0, pl.ds(o, NY, stride=NB), :] = current[4]
        zst[1, pl.ds(o, NY, stride=NB), :] = current[5]
        y_ref[o] = jnp.concatenate([current[4], current[5]], axis=0).astype(BF16)
        return current[4], current[5]

    def filter_pair(i, _):
        low0, high0 = filter_one(2 * i)
        low1, high1 = filter_one(2 * i + 1)
        halo_out[0, i] = jnp.concatenate([low0, low1], axis=0).astype(BF16)
        halo_out[1, i] = jnp.concatenate([high0, high1], axis=0).astype(BF16)
        return 0

    me = 32 * b
    mate = 32 * (x * 2 + (1 - h))
    x_steps = (1, -1, 2)
    half = NB // HALVES
    band_in, fwd_in, mate_in = [], [], []
    for t in range(HALVES):
        for c in range(t * CHUNKS // HALVES, (t + 1) * CHUNKS // HALVES):
            for cp in x_in[c]:
                cp.wait_recv()
            lax.fori_loop(c * size // 2, (c + 1) * size // 2, filter_pair, 0)
        rows = pl.ds(pl.multiple_of(me + t * half, 16), half)
        for y in range(NY):
            for p in range(2):
                piece = zst[p, y * NB + t * half:y * NB + (t + 1) * half, :].astype(BF16)
                zall[y, rows, p * NZ:(p + 1) * NZ] = piece
                lhs[y, t * half:(t + 1) * half, p * NZ:(p + 1) * NZ] = piece
        piece = zall.at[:, rows, :]
        cp = remote(piece, piece, bss.at[0, t], brs.at[0, t], at_b(0, 1))
        cp.start()
        mate_in.append(cp)
        for n, s in enumerate(x_steps):
            cp = remote(piece, piece, bss.at[n + 1, t], brs.at[n + 1, t], at_b(s, 0))
            cp.start()
            band_in.append(cp)
    pending += mate_in + band_in

    h_in = []
    for n, s in enumerate((-1, 1)):
        cp = remote(halo_out.at[n], halo_in.at[1 - n], hss.at[n], hrs.at[n], at_d(s))
        cp.start()
        h_in.append(cp)
    pending += h_in

    for t in range(HALVES):
        mate_in[t].wait_recv()
        piece = zall.at[:, pl.ds(pl.multiple_of(mate + t * half, 16), half), :]
        for n, s in enumerate(x_steps):
            cp = remote(piece, piece, fss.at[n, t], frs.at[n, t], at_b(s, 0))
            cp.start()
            fwd_in.append(cp)
    pending += fwd_in

    for cp in h_in:
        cp.wait_recv()

    def apply_pair(i, _):
        left, right = halo_in[0, i].astype(F32), halo_in[1, i].astype(F32)
        for q in range(2):
            o = 2 * i + q
            block = y_ref[o].astype(F32)
            planes = (left[q * NY:(q + 1) * NY], block[:NY], block[NY:], right[q * NY:(q + 1) * NY])
            for p in (1, 2):
                near = (planes[p - 1] + planes[p + 1]) + side_sum(planes[p])
                value = -0.5 * (near - 6.0 * planes[p]) + v_ref[(p - 1) * NY:p * NY, :] * planes[p]
                hst[p - 1, pl.ds(o, NY, stride=NB), :] = value
        return 0

    lax.fori_loop(0, NB // 2, apply_pair, 0)
    for y in range(NY):
        for p in range(2):
            lhs[y, NB:2 * NB, p * NZ:(p + 1) * NZ] = hst[p, y * NB:(y + 1) * NB, :].astype(BF16)

    for cp in band_in + fwd_in:
        cp.wait_recv()
    total = None
    for y in range(NY):
        term = lax.dot_general(lhs[y], zall[y], (((1,), (1,)), ((), ())), preferred_element_type=F32)
        total = term if total is None else total + term
    gsum[...] = total

    r_in = []
    for s in range(1, GROUP):
        there = lax.rem(j + s, GROUP)
        cp = remote(gsum.at[pl.ds(pl.multiple_of(there * 8, 8), 8)], rsb.at[s], rss.at[s], rrs.at[s], at_g(s))
        cp.start()
        r_in.append(cp)
    pending += r_in
    mine = pl.ds(pl.multiple_of(j * 8, 8), 8)
    shard = gsum[mine, :]
    for s in range(1, GROUP):
        r_in[s - 1].wait_recv()
        shard = shard + rsb[s]
    zb[z] = shard

    up, down = n_z // 2, (n_z - 1) // 2

    def hop(way, k):
        origin = lax.rem(z - way * k + n_z, n_z)
        n = (way + 1) // 2
        cp = remote(zb.at[origin], zb.at[origin], zss.at[n, k], zrs.at[n, k], at_z(way))
        cp.start()
        return cp

    ups, downs = [hop(1, 0)], [hop(-1, 0)]
    for k in range(1, up):
        ups[-1].wait_recv()
        ups.append(hop(1, k))
    for k in range(1, down):
        downs[-1].wait_recv()
        downs.append(hop(-1, k))
    ups[-1].wait_recv()
    downs[-1].wait_recv()
    pending += ups + downs
    values = [zb[k] for k in range(n_z)]
    while len(values) > 1:
        values = [values[k] + values[k + 1] for k in range(0, len(values), 2)]
    fin[mine, :] = values[0] * scale

    a_in = []
    for s in range(1, GROUP):
        cp = remote(fin.at[mine], fin.at[mine], ass.at[s], ars.at[s], at_g(s))
        cp.start()
        a_in.append(cp)
    for cp in a_in:
        cp.wait_recv()
    pending += a_in
    g_ref[...] = fin[...]
    for cp in pending:
        cp.wait_send()


def shards(orbitals, potential, n_domain, n_band):
    n_z = n_domain // GROUP
    half_z = n_z // 2
    block = orbitals.reshape(NB, 2 * NY, NZ)
    scale = 1.0 / (n_domain * 2 * NY * NZ)
    dma = pltpu.SemaphoreType.DMA
    vmem = pl.BlockSpec(memory_space=pltpu.VMEM)
    filtered, rows = pl.pallas_call(
        functools.partial(kernel, n_domain, scale),
        out_shape=(
            jax.ShapeDtypeStruct((NB, 2 * NY, NZ), BF16),
            jax.ShapeDtypeStruct((2 * NB, n_band * NB), F32),
        ),
        in_specs=[pl.BlockSpec(memory_space=pl.ANY), vmem],
        out_specs=(vmem, vmem),
        scratch_shapes=[
            pltpu.VMEM((5, NB, 2 * NY, NZ), BF16),
            pltpu.VMEM((5, 2 * NY, NZ), F32),
            pltpu.VMEM((4, 10, NY, NZ), F32),
            pltpu.VMEM((2, NY * NB, NZ), F32),
            pltpu.VMEM((2, NY * NB, NZ), F32),
            pltpu.VMEM((2, NB // 2, 2 * NY, NZ), BF16),
            pltpu.VMEM((2, NB // 2, 2 * NY, NZ), BF16),
            pltpu.VMEM((NY, n_band * NB, 2 * NZ), BF16),
            pltpu.VMEM((NY, 2 * NB, 2 * NZ), BF16),
            pltpu.VMEM((2 * NB, n_band * NB), F32),
            pltpu.VMEM((GROUP, 8, n_band * NB), F32),
            pltpu.VMEM((n_z, 8, n_band * NB), F32),
            pltpu.VMEM((2 * NB, n_band * NB), F32),
            dma,
            dma((4, CHUNKS)), dma((4, CHUNKS)),
            dma((4,)), dma((4,)),
            dma((2,)), dma((2,)),
            dma((4, HALVES)), dma((4, HALVES)),
            dma((3, HALVES)), dma((3, HALVES)),
            dma((GROUP,)), dma((GROUP,)),
            dma((2, half_z)), dma((2, half_z)),
            dma((GROUP,)), dma((GROUP,)),
        ],
        compiler_params=pltpu.CompilerParams(
            collective_id=1, has_side_effects=True, vmem_limit_bytes=24 * 1024 * 1024
        ),
    )(block, potential.reshape(2 * NY, NZ))
    return filtered.reshape(orbitals.shape), rows[:NB], rows[NB:]


def solution(mesh):
    body = functools.partial(shards, n_domain=mesh.shape["domain"], n_band=mesh.shape["band"])
    in_specs = (P("band", "domain", None, None), P("domain", None, None))
    out_specs = (P("band", "domain", None, None), P("band", None), P("band", None))
    return jax.shard_map(body, mesh=mesh, in_specs=in_specs, out_specs=out_specs, check_vma=False)
```

time: 1070 us -> 97.5 us (0.09)
  waiting for transfers between devices: 979 us -> 0 us
  Pallas kernels: 0 us -> 93.8 us
  starting transfers between devices: 60.2 us -> 0 us
  between operations: 14.4 us -> 0.65 us
    psum x1 -> x0, waiting for transfers between devices: 909 us -> none  [shards(): over_sum, proj_sum = lax.psum((over_tile, proj_tile), 'domain')]
    pallas_call x0 -> x1, Pallas kernels: none -> 93.8 us  [shards(): pl.pallas_call(functools.partial(kernel, n_domain, scale), out_shape=(jax...]
    ppermute x10 -> x0, starting transfers between devices: 60.1 us -> none  [the longest x5 50.5 us: extended_2(): lax.ppermute(lax.slice_in_dim(block, 0, width, axis=dim), axis, backward)]
    all_gather x1 -> x0, waiting for transfers between devices: 58.6 us -> none  [shards(): piece = lax.all_gather(filtered, 'band', axis=0, tiled=True)]
    ppermute x10 -> x0, waiting for transfers between devices: 11.6 us -> none  [the longest x5 11.6 us: extended_2(): lax.ppermute(lax.slice_in_dim(block, block.shape[dim] - width, None, axis...]
  transfers between devices with their start and end apart: 12 -> 0, of which waited for: 6 -> 0; matrix products, arithmetic and copies ran while one was open for 0% -> 0% of each run, Pallas kernels for 0% -> 0%
where the time goes in v1:
time: 97.5 us; the launch traced here: 97.3 us
  Pallas kernels  93.8 us (96%)
  local copies, waits for them, and re-layouts  2.88 us (3%)
    pallas_call x1, Pallas kernels, shards(): pl.pallas_call(functools.partial(kernel, n_domain, scale), out_shape=(jax...  93.8 us
    unnamed x5, local copies, waits for them, and re-layouts  2.25 us

profile of v1, /device:TPU:1, one launch (start us, length us, event | category | flops | bytes accessed | tf_op | source)
XLA Modules:
  0.0 97.3 jit_solution(15230136606749302279)
XLA Ops:
  0.6 0.0 copy-start
  0.6 0.9 copy-done
  1.5 0.0 copy-start.1
  1.5 0.7 copy-done.1
  2.2 93.8 %shard_map.49 = (bf16[32,16,128]{2,1,0:T(8,128)(2,1)S(1)}, f32[64,256]{1,0:T(8,128)S(1)}) custom-call(bf16[32,16,128]{2,1,0:T(8,128)(2,1)S(1)} %bitcast.3, f32[16,128]{1,0:T(8,128)S(1)} %bitcast.5), custom_call_target="tpu_custom_call" | custom-call | tf_op jit(solution)/shard_map/pallas_call | solution.py:269
  96.0 0.6 fusion
  96.6 0.7 copy.6
Async XLA Ops:
  0.6 0.9 copy-start
  1.5 0.7 copy-start.1

commit v2 on v1

--- a/solution.py
+++ b/solution.py
@@ -19,6 +19,7 @@
 NZ = 128
 CHUNKS = 4
 HALVES = 2
+BATCH = 4
 
 
 def filter_terms():
@@ -43,10 +44,10 @@
 
 def kernel(
     n_domain, scale,
-    x_hbm, v_ref,
+    x_hbm, v_hbm,
     y_ref, g_ref,
     xs, vs, ws, zst, hst, halo_out, halo_in, zall, lhs, gsum, rsb, zb, fin,
-    lsem, xss, xrs, vss, vrs, hss, hrs, bss, brs, fss, frs, rss, rrs, zss, zrs, ass, ars,
+    lsem, xss, xrs, vss, vrs, hss, hrs, bss, brs, fss, frs, rss, rrs, zss, zrs, ass, ars, tokens,
 ):
     n_z = n_domain // GROUP
     d = lax.axis_index("domain")
@@ -71,16 +72,27 @@
             src_ref=src, dst_ref=dst, send_sem=send, recv_sem=recv, device_id=to, device_id_type=MESH
         )
 
-    own = pltpu.make_async_copy(x_hbm, xs.at[2], lsem)
+    own = pltpu.make_async_copy(x_hbm, xs.at[2], lsem.at[0])
+    own_v = pltpu.make_async_copy(v_hbm, vs.at[2], lsem.at[1])
     own.start()
+    own_v.start()
     barrier = pltpu.get_barrier_semaphore()
     partners = [at_d(s) for s in (-2, -1, 1, 2)] + [at_g(s) for s in range(1, GROUP)] + [at_z(-1), at_z(1)]
     partners += [at_b(0, 1), at_b(1, 0), at_b(-1, 0), at_b(2, 0)]
     for to in partners:
         pl.semaphore_signal(barrier, inc=1, device_id=to, device_id_type=MESH)
-    vs[2] = v_ref[...]
     own.wait()
+    own_v.wait()
     pl.semaphore_wait(barrier, len(partners))
+
+    def greet(n):
+        for to in (at_z(-(1 << n)), at_z(1 << n)):
+            pl.semaphore_signal(tokens.at[n], inc=1, device_id=to, device_id_type=MESH)
+
+    def greeted(n):
+        pl.semaphore_wait(tokens.at[n], 2)
+
+    greet(0)
 
     pending = []
     shifts = (-1, 1, -2, 2)
@@ -108,34 +120,37 @@
         for p in range(k + 1, 9 - k):
             ws[k, p] = alpha * (vs[p // 2, (p % 2) * NY:(p % 2) * NY + NY, :] + (3.0 - center))
 
-    def filter_one(o):
-        prior = {}
-        for s in range(5):
-            block = xs[s, o].astype(F32)
-            prior[2 * s], prior[2 * s + 1] = block[:NY], block[NY:]
-        current = None
+    def filter_some(i, _):
+        orbitals = [i * BATCH + q for q in range(BATCH)]
+        priors, currents = [], [None] * BATCH
+        for o in orbitals:
+            planes = {}
+            for s in range(5):
+                block = xs[s, o].astype(F32)
+                planes[2 * s], planes[2 * s + 1] = block[:NY], block[NY:]
+            priors.append(planes)
         for k, (alpha, beta) in enumerate(terms):
-            base = prior if k == 0 else current
-            update = {}
-            for p in range(k + 1, 9 - k):
-                near = side_sum(base[p]) + (base[p - 1] + base[p + 1])
-                value = ws[k, p] * base[p] - (0.5 * alpha) * near
+            for q in range(BATCH):
+                base = currents[q] if k else priors[q]
+                update = {}
+                for p in range(k + 1, 9 - k):
+                    near = side_sum(base[p]) + (base[p - 1] + base[p + 1])
+                    value = ws[k, p] * base[p] - (0.5 * alpha) * near
+                    if k:
+                        value = value - beta * priors[q][p]
+                    update[p] = value
                 if k:
-                    value = value - beta * prior[p]
-                update[p] = value
-            if k:
-                prior = current
-            current = update
-        zst[0, pl.ds(o, NY, stride=NB), :] = current[4]
-        zst[1, pl.ds(o, NY, stride=NB), :] = current[5]
-        y_ref[o] = jnp.concatenate([current[4], current[5]], axis=0).astype(BF16)
-        return current[4], current[5]
-
-    def filter_pair(i, _):
-        low0, high0 = filter_one(2 * i)
-        low1, high1 = filter_one(2 * i + 1)
-        halo_out[0, i] = jnp.concatenate([low0, low1], axis=0).astype(BF16)
-        halo_out[1, i] = jnp.concatenate([high0, high1], axis=0).astype(BF16)
+                    priors[q] = currents[q]
+                currents[q] = update
+        for q, o in enumerate(orbitals):
+            low, high = currents[q][4], currents[q][5]
+            zst[0, pl.ds(o, NY, stride=NB), :] = low
+            zst[1, pl.ds(o, NY, stride=NB), :] = high
+            y_ref[o] = jnp.concatenate([low, high], axis=0).astype(BF16)
+        for q in range(0, BATCH, 2):
+            for side in range(2):
+                pair = [currents[q + r][4 + side] for r in range(2)]
+                halo_out[side, i * (BATCH // 2) + q // 2] = jnp.concatenate(pair, axis=0).astype(BF16)
         return 0
 
     me = 32 * b
@@ -147,7 +162,7 @@
         for c in range(t * CHUNKS // HALVES, (t + 1) * CHUNKS // HALVES):
             for cp in x_in[c]:
                 cp.wait_recv()
-            lax.fori_loop(c * size // 2, (c + 1) * size // 2, filter_pair, 0)
+            lax.fori_loop(c * size // BATCH, (c + 1) * size // BATCH, filter_some, 0)
         rows = pl.ds(pl.multiple_of(me + t * half, 16), half)
         for y in range(NY):
             for p in range(2):
@@ -171,6 +186,8 @@
         h_in.append(cp)
     pending += h_in
 
+    greeted(0)
+    greet(1)
     for t in range(HALVES):
         mate_in[t].wait_recv()
         piece = zall.at[:, pl.ds(pl.multiple_of(mate + t * half, 16), half), :]
@@ -191,7 +208,7 @@
             planes = (left[q * NY:(q + 1) * NY], block[:NY], block[NY:], right[q * NY:(q + 1) * NY])
             for p in (1, 2):
                 near = (planes[p - 1] + planes[p + 1]) + side_sum(planes[p])
-                value = -0.5 * (near - 6.0 * planes[p]) + v_ref[(p - 1) * NY:p * NY, :] * planes[p]
+                value = -0.5 * (near - 6.0 * planes[p]) + vs[2, (p - 1) * NY:p * NY, :] * planes[p]
                 hst[p - 1, pl.ds(o, NY, stride=NB), :] = value
         return 0
 
@@ -200,6 +217,8 @@
         for p in range(2):
             lhs[y, NB:2 * NB, p * NZ:(p + 1) * NZ] = hst[p, y * NB:(y + 1) * NB, :].astype(BF16)
 
+    greeted(1)
+    greet(2)
     for cp in band_in + fwd_in:
         cp.wait_recv()
     total = None
@@ -222,25 +241,15 @@
         shard = shard + rsb[s]
     zb[z] = shard
 
-    up, down = n_z // 2, (n_z - 1) // 2
-
-    def hop(way, k):
-        origin = lax.rem(z - way * k + n_z, n_z)
-        n = (way + 1) // 2
-        cp = remote(zb.at[origin], zb.at[origin], zss.at[n, k], zrs.at[n, k], at_z(way))
-        cp.start()
-        return cp
-
-    ups, downs = [hop(1, 0)], [hop(-1, 0)]
-    for k in range(1, up):
-        ups[-1].wait_recv()
-        ups.append(hop(1, k))
-    for k in range(1, down):
-        downs[-1].wait_recv()
-        downs.append(hop(-1, k))
-    ups[-1].wait_recv()
-    downs[-1].wait_recv()
-    pending += ups + downs
+    greeted(2)
+    z_in = []
+    for s in sorted(range(1, n_z), key=lambda s: -min(s, n_z - s)):
+        cp = remote(zb.at[z], zb.at[z], zss.at[s], zrs.at[s], at_z(s))
+        cp.start()
+        z_in.append(cp)
+    for cp in z_in:
+        cp.wait_recv()
+    pending += z_in
     values = [zb[k] for k in range(n_z)]
     while len(values) > 1:
         values = [values[k] + values[k + 1] for k in range(0, len(values), 2)]
@@ -261,7 +270,6 @@
 
 def shards(orbitals, potential, n_domain, n_band):
     n_z = n_domain // GROUP
-    half_z = n_z // 2
     block = orbitals.reshape(NB, 2 * NY, NZ)
     scale = 1.0 / (n_domain * 2 * NY * NZ)
     dma = pltpu.SemaphoreType.DMA
@@ -272,7 +280,7 @@
             jax.ShapeDtypeStruct((NB, 2 * NY, NZ), BF16),
             jax.ShapeDtypeStruct((2 * NB, n_band * NB), F32),
         ),
-        in_specs=[pl.BlockSpec(memory_space=pl.ANY), vmem],
+        in_specs=[pl.BlockSpec(memory_space=pltpu.HBM)] * 2,
         out_specs=(vmem, vmem),
         scratch_shapes=[
             pltpu.VMEM((5, NB, 2 * NY, NZ), BF16),
@@ -288,15 +296,16 @@
             pltpu.VMEM((GROUP, 8, n_band * NB), F32),
             pltpu.VMEM((n_z, 8, n_band * NB), F32),
             pltpu.VMEM((2 * NB, n_band * NB), F32),
-            dma,
+            dma((2,)),
             dma((4, CHUNKS)), dma((4, CHUNKS)),
             dma((4,)), dma((4,)),
             dma((2,)), dma((2,)),
             dma((4, HALVES)), dma((4, HALVES)),
             dma((3, HALVES)), dma((3, HALVES)),
             dma((GROUP,)), dma((GROUP,)),
-            dma((2, half_z)), dma((2, half_z)),
+            dma((n_z,)), dma((n_z,)),
             dma((GROUP,)), dma((GROUP,)),
+            pltpu.SemaphoreType.REGULAR((3,)),
         ],
         compiler_params=pltpu.CompilerParams(
             collective_id=1, has_side_effects=True, vmem_limit_bytes=24 * 1024 * 1024

time: 97.5 us -> 68.7 us (0.70)
  Pallas kernels: 93.8 us -> 65 us
    pallas_call x1, Pallas kernels: 93.8 us -> 65 us  [shards(): pl.pallas_call(functools.partial(kernel, n_domain, scale), out_shape=(jax...]
where the time goes in v2:
time: 68.7 us; the launch traced here: 68.5 us
  Pallas kernels  65 us (95%)
  local copies, waits for them, and re-layouts  2.88 us (4%)
    pallas_call x1, Pallas kernels, shards(): pl.pallas_call(functools.partial(kernel, n_domain, scale), out_shape=(jax...  65 us
    unnamed x5, local copies, waits for them, and re-layouts  2.25 us

profile of v2, /device:TPU:1, one launch (start us, length us, event | category | flops | bytes accessed | tf_op | source)
XLA Modules:
  0.0 68.5 jit_solution(17702618472016854246)
XLA Ops:
  0.6 0.0 copy-start
  0.6 0.9 %copy-done = bf16[32,2,8,128]{3,2,1,0:T(8,128)(2,1)S(1)} copy-done((bf16[32,2,8,128]{3,2,1,0:T(8,128)(2,1)S(1)}, bf16[32,2,8,128]{3,2,1,0:T(8,128)(2,1)}, u32[]{:S(2)}) %copy-start) | copy-done | bytes 131096
  1.5 0.0 copy-start.1
  1.5 0.7 %copy-done.1 = f32[2,8,128]{2,1,0:T(8,128)S(1)} copy-done((f32[2,8,128]{2,1,0:T(8,128)S(1)}, f32[2,8,128]{2,1,0:T(8,128)}, u32[]{:S(2)}) %copy-start.1) | copy-done | bytes 8216
  2.2 65.0 %shard_map.49 = (bf16[32,16,128]{2,1,0:T(8,128)(2,1)S(1)}, f32[64,256]{1,0:T(8,128)S(1)}) custom-call(bf16[32,16,128]{2,1,0:T(8,128)(2,1)S(1)} %bitcast.3, f32[16,128]{1,0:T(8,128)S(1)} %bitcast.5), custom_call_target="tpu_custom_call" | custom-call | tf_op jit(solution)/shard_map/pallas_call | solution.py:277
  67.2 0.6 fusion
  67.8 0.7 copy.6
Async XLA Ops:
  0.6 0.9 %copy-start = (bf16[32,2,8,128]{3,2,1,0:T(8,128)(2,1)S(1)}, bf16[32,2,8,128]{3,2,1,0:T(8,128)(2,1)}, u32[]{:S(2)}) copy-start(bf16[32,2,8,128]{3,2,1,0:T(8,128)(2,1)} %param.2) | copy-start | bytes 393220
  1.5 0.7 %copy-start.1 = (f32[2,8,128]{2,1,0:T(8,128)S(1)}, f32[2,8,128]{2,1,0:T(8,128)}, u32[]{:S(2)}) copy-start(f32[2,8,128]{2,1,0:T(8,128)} %param.3) | copy-start | bytes 24580

commit v3 on v2

--- a/solution.py
+++ b/solution.py
@@ -19,6 +19,8 @@
 NZ = 128
 CHUNKS = 4
 HALVES = 2
+SPLIT = 2
+MATE_FIRST = False
 BATCH = 4
 
 
@@ -158,6 +160,11 @@
     x_steps = (1, -1, 2)
     half = NB // HALVES
     band_in, fwd_in, mate_in = [], [], []
+
+    def band_piece(start, t, u):
+        rows = pl.ds(pl.multiple_of(start + t * half, 16), half)
+        return zall.at[u * (NY // SPLIT):(u + 1) * (NY // SPLIT), rows, :]
+
     for t in range(HALVES):
         for c in range(t * CHUNKS // HALVES, (t + 1) * CHUNKS // HALVES):
             for cp in x_in[c]:
@@ -169,14 +176,20 @@
                 piece = zst[p, y * NB + t * half:y * NB + (t + 1) * half, :].astype(BF16)
                 zall[y, rows, p * NZ:(p + 1) * NZ] = piece
                 lhs[y, t * half:(t + 1) * half, p * NZ:(p + 1) * NZ] = piece
-        piece = zall.at[:, rows, :]
-        cp = remote(piece, piece, bss.at[0, t], brs.at[0, t], at_b(0, 1))
-        cp.start()
-        mate_in.append(cp)
-        for n, s in enumerate(x_steps):
-            cp = remote(piece, piece, bss.at[n + 1, t], brs.at[n + 1, t], at_b(s, 0))
+        for u in range(SPLIT):
+            piece = band_piece(me, t, u)
+            cp = remote(piece, piece, bss.at[0, t, u], brs.at[0, t, u], at_b(0, 1))
             cp.start()
-            band_in.append(cp)
+            mate_in.append(cp)
+        if MATE_FIRST and t < HALVES - 1:
+            continue
+        for tt in range(HALVES) if MATE_FIRST else (t,):
+            for u in range(SPLIT):
+                piece = band_piece(me, tt, u)
+                for n, s in enumerate(x_steps):
+                    cp = remote(piece, piece, bss.at[n + 1, tt, u], brs.at[n + 1, tt, u], at_b(s, 0))
+                    cp.start()
+                    band_in.append(cp)
     pending += mate_in + band_in
 
     h_in = []
@@ -189,12 +202,13 @@
     greeted(0)
     greet(1)
     for t in range(HALVES):
-        mate_in[t].wait_recv()
-        piece = zall.at[:, pl.ds(pl.multiple_of(mate + t * half, 16), half), :]
-        for n, s in enumerate(x_steps):
-            cp = remote(piece, piece, fss.at[n, t], frs.at[n, t], at_b(s, 0))
-            cp.start()
-            fwd_in.append(cp)
+        for u in range(SPLIT):
+            mate_in[t * SPLIT + u].wait_recv()
+            piece = band_piece(mate, t, u)
+            for n, s in enumerate(x_steps):
+                cp = remote(piece, piece, fss.at[n, t, u], frs.at[n, t, u], at_b(s, 0))
+                cp.start()
+                fwd_in.append(cp)
     pending += fwd_in
 
     for cp in h_in:
@@ -239,7 +253,7 @@
     for s in range(1, GROUP):
         r_in[s - 1].wait_recv()
         shard = shard + rsb[s]
-    zb[z] = shard
+    zb[z] = jnp.concatenate([shard[:, :128], shard[:, 128:]], axis=0).astype(BF16)
 
     greeted(2)
     z_in = []
@@ -250,10 +264,11 @@
     for cp in z_in:
         cp.wait_recv()
     pending += z_in
-    values = [zb[k] for k in range(n_z)]
+    values = [zb[k].astype(F32) for k in range(n_z)]
     while len(values) > 1:
         values = [values[k] + values[k + 1] for k in range(0, len(values), 2)]
-    fin[mine, :] = values[0] * scale
+    result = values[0] * scale
+    fin[mine, :] = jnp.concatenate([result[:8], result[8:]], axis=1)
 
     a_in = []
     for s in range(1, GROUP):
@@ -294,14 +309,14 @@
             pltpu.VMEM((NY, 2 * NB, 2 * NZ), BF16),
             pltpu.VMEM((2 * NB, n_band * NB), F32),
             pltpu.VMEM((GROUP, 8, n_band * NB), F32),
-            pltpu.VMEM((n_z, 8, n_band * NB), F32),
+            pltpu.VMEM((n_z, 16, n_band * NB // 2), BF16),
             pltpu.VMEM((2 * NB, n_band * NB), F32),
             dma((2,)),
             dma((4, CHUNKS)), dma((4, CHUNKS)),
             dma((4,)), dma((4,)),
             dma((2,)), dma((2,)),
-            dma((4, HALVES)), dma((4, HALVES)),
-            dma((3, HALVES)), dma((3, HALVES)),
+            dma((4, HALVES, SPLIT)), dma((4, HALVES, SPLIT)),
+            dma((3, HALVES, SPLIT)), dma((3, HALVES, SPLIT)),
             dma((GROUP,)), dma((GROUP,)),
             dma((n_z,)), dma((n_z,)),
             dma((GROUP,)), dma((GROUP,)),
@@ -310,7 +325,7 @@
         compiler_params=pltpu.CompilerParams(
             collective_id=1, has_side_effects=True, vmem_limit_bytes=24 * 1024 * 1024
         ),
-    )(block, potential.reshape(2 * NY, NZ))
+    )(*(pltpu.with_memory_space_constraint(a, pltpu.HBM) for a in (block, potential.reshape(2 * NY, NZ))))
     return filtered.reshape(orbitals.shape), rows[:NB], rows[NB:]
 
 

time: 68.7 us -> 63.8 us (0.929)
  Pallas kernels: 65 us -> 61.7 us
  local copies, waits for them, and re-layouts: 2.88 us -> 1.29 us
    pallas_call x1, Pallas kernels: 65 us -> 61.7 us  [shards(): pl.pallas_call(functools.partial(kernel, n_domain, scale), out_shape=(jax...]
    unnamed x5 -> x1, local copies, waits for them, and re-layouts: 2.25 us -> 0.65 us
where the time goes in v3:
time: 63.8 us; the launch traced here: 63.7 us
  Pallas kernels  61.7 us (97%)
  local copies, waits for them, and re-layouts  1.29 us (2%)
  between operations  0.64 us (1%)
    pallas_call x1, Pallas kernels, shards(): pl.pallas_call(functools.partial(kernel, n_domain, scale), out_shape=(jax...  61.7 us

profile of v3, /device:TPU:1, one launch (start us, length us, event | category | flops | bytes accessed | tf_op | source)
XLA Modules:
  0.0 63.7 jit_solution(15692159036822934934)
XLA Ops:
  0.6 61.7 %shard_map.49 = (bf16[32,16,128]{2,1,0:T(8,128)(2,1)S(1)}, f32[64,256]{1,0:T(8,128)S(1)}) custom-call(bf16[32,16,128]{2,1,0:T(8,128)(2,1)} %bitcast.4, f32[16,128]{1,0:T(8,128)} %bitcast.5), custom_call_target="tpu_custom_call" | custom-call | tf_op jit(solution)/shard_map/pallas_call | solution.py:292
  62.4 0.6 fusion
  63.0 0.7 %copy.6 = bf16[32,2,8,128]{3,2,1,0:T(8,128)(2,1)} copy(bf16[32,2,8,128]{3,2,1,0:T(8,128)(2,1)S(1)} %bitcast.3) | data formatting | bytes 262144

commit v4 on v3

--- a/solution.py
+++ b/solution.py
@@ -48,7 +48,7 @@
     n_domain, scale,
     x_hbm, v_hbm,
     y_ref, g_ref,
-    xs, vs, ws, zst, hst, halo_out, halo_in, zall, lhs, gsum, rsb, zb, fin,
+    xs, vs, ws, zst, hst, halo_out, halo_in, zall, lhs, gsum, gsend, rsb, zb, fin,
     lsem, xss, xrs, vss, vrs, hss, hrs, bss, brs, fss, frs, rss, rrs, zss, zrs, ass, ars, tokens,
 ):
     n_z = n_domain // GROUP
@@ -239,21 +239,25 @@
     for y in range(NY):
         term = lax.dot_general(lhs[y], zall[y], (((1,), (1,)), ((), ())), preferred_element_type=F32)
         total = term if total is None else total + term
-    gsum[...] = total
+    for k in range(GROUP):
+        rows = total[8 * k:8 * k + 8]
+        packed = jnp.concatenate([rows[:, :128], rows[:, 128:]], axis=0)
+        gsum[k] = packed
+        gsend[k] = packed.astype(BF16)
 
     r_in = []
     for s in range(1, GROUP):
         there = lax.rem(j + s, GROUP)
-        cp = remote(gsum.at[pl.ds(pl.multiple_of(there * 8, 8), 8)], rsb.at[s], rss.at[s], rrs.at[s], at_g(s))
+        cp = remote(gsend.at[there], rsb.at[s], rss.at[s], rrs.at[s], at_g(s))
         cp.start()
         r_in.append(cp)
     pending += r_in
     mine = pl.ds(pl.multiple_of(j * 8, 8), 8)
-    shard = gsum[mine, :]
+    shard = gsum[j]
     for s in range(1, GROUP):
         r_in[s - 1].wait_recv()
-        shard = shard + rsb[s]
-    zb[z] = jnp.concatenate([shard[:, :128], shard[:, 128:]], axis=0).astype(BF16)
+        shard = shard + rsb[s].astype(F32)
+    zb[z] = shard.astype(BF16)
 
     greeted(2)
     z_in = []
@@ -307,8 +311,9 @@
             pltpu.VMEM((2, NB // 2, 2 * NY, NZ), BF16),
             pltpu.VMEM((NY, n_band * NB, 2 * NZ), BF16),
             pltpu.VMEM((NY, 2 * NB, 2 * NZ), BF16),
-            pltpu.VMEM((2 * NB, n_band * NB), F32),
-            pltpu.VMEM((GROUP, 8, n_band * NB), F32),
+            pltpu.VMEM((GROUP, 16, n_band * NB // 2), F32),
+            pltpu.VMEM((GROUP, 16, n_band * NB // 2), BF16),
+            pltpu.VMEM((GROUP, 16, n_band * NB // 2), BF16),
             pltpu.VMEM((n_z, 16, n_band * NB // 2), BF16),
             pltpu.VMEM((2 * NB, n_band * NB), F32),
             dma((2,)),

time: 63.8 us -> 63.6 us (level)
  no operation moved by 1% of the time
where the time goes in v4:
time: 63.6 us; the launch traced here: 63.4 us
  Pallas kernels  61.5 us (97%)
  local copies, waits for them, and re-layouts  1.29 us (2%)
  between operations  0.64 us (1%)
    pallas_call x1, Pallas kernels, shards(): pl.pallas_call(functools.partial(kernel, n_domain, scale), out_shape=(jax...  61.5 us

profile of v4, /device:TPU:1, one launch (start us, length us, event | category | flops | bytes accessed | tf_op | source)
XLA Modules:
  0.0 63.4 jit_solution(4801110453579578749)
XLA Ops:
  0.6 61.5 %shard_map.49 = (bf16[32,16,128]{2,1,0:T(8,128)(2,1)S(1)}, f32[64,256]{1,0:T(8,128)S(1)}) custom-call(bf16[32,16,128]{2,1,0:T(8,128)(2,1)} %bitcast.4, f32[16,128]{1,0:T(8,128)} %bitcast.5), custom_call_target="tpu_custom_call" | custom-call | tf_op jit(solution)/shard_map/pallas_call | solution.py:296
  62.1 0.6 fusion
  62.7 0.7 %copy.6 = bf16[32,2,8,128]{3,2,1,0:T(8,128)(2,1)} copy(bf16[32,2,8,128]{3,2,1,0:T(8,128)(2,1)S(1)} %bitcast.3) | data formatting | bytes 262144
